TPU v7x, 32 devices: a whole 2x2x4 slice. The times are simulated.
32 devices in a mesh: grp: 4 (over z), seq: 8 (over y, x, core).
Axes of the slice: x: 2, y: 2, z: 4, core: 2. Of those that a mesh axis runs over, the one named last changes fastest.
Arguments:
- queries: bfloat16 [4096, 6144], P(('grp', 'seq')), may hold values from -64 to 64
- keys_values: bfloat16 [4096, 768], P(('grp', 'seq')), may hold values from -6 to 6
- selection: int32 [64, 32], P(('grp', 'seq')), may hold values from -1 to 63, as said below
- gate_logits: bfloat16 [3, 4096, 32], P(None, ('grp', 'seq')), may hold values from -6 to 6
- pos_weight: bfloat16 [64, 384], replicated, may hold values from -0.75 to 0.75
- compress_weight: bfloat16 [384, 384], replicated, may hold values from -0.3125 to 0.3125
Outputs:
- attended: bfloat16 [4096, 6144], P(('grp', 'seq'))
Inputs may be any that keep to these rules, and one draw needn't show every extreme that they name: `selection`: A run is the 2 rows of one device; a segment is 16 consecutive rows. Row r lists, for each group, 16 distinct block numbers no greater than r, or -1 for unused entries. Within one group, the rows of a run list from each earlier segment exactly one block, and it lies in the run at the same place of that segment; from any other run of their own segment they list at most one block.
All inputs are finite; a program needn't handle non-finite values.
Results may differ from a plain program's by a relative error of at most 0.0055.
Values may be sent and summed in bfloat16 or wider, within the bound.
A program may use at most 128 MiB of HBM per device.

v0:
```python
import math
import jax
import jax.numpy as jnp
from jax import lax
from jax.sharding import PartitionSpec as P

HEAD_DIM = 192
GROUPS = 2
GROUP_HEADS = 16
HEADS = 32
BLOCK = 64
TOP = 16
CAP = 2
WINDOW = 128
NEG_FILL = -1e30


def from_behind(block, axis, distance):
    devices = range(lax.axis_size(axis))
    route = [(i - distance, i) for i in devices if i - distance in devices]
    return lax.ppermute(block, axis, route)


def attend(query_block, key_block, allowed, with_sink):
    head_dim = query_block.shape[-1]
    score_scale = head_dim ** (-0.5)
    scores = (
        jnp.einsum(
            "btghd,bgnd->bghtn",
            query_block,
            key_block[..., :head_dim],
            preferred_element_type=jnp.float32,
        )
        * score_scale
    )
    allowed_wide = allowed[:, :, None]
    scores = jnp.where(allowed_wide, scores, NEG_FILL)
    top_score = jnp.max(scores, axis=-1, keepdims=True)
    if with_sink:
        top_score = jnp.maximum(top_score, 0.0)
    weights = jnp.where(allowed_wide, jnp.exp(scores - top_score), 0.0)
    denominator = jnp.sum(weights, axis=-1, keepdims=True)
    if with_sink:
        denominator = denominator + jnp.exp(-top_score)
    rounded = weights.astype(jnp.bfloat16)
    blended = (
        jnp.einsum(
            "bghtn,bgnd->bghtd",
            rounded,
            key_block[..., head_dim:],
            preferred_element_type=jnp.float32,
        )
        / denominator
    )
    return jnp.transpose(blended, (0, 3, 1, 2, 4))


def by_heads(query_block, key_block, allowed, with_sink):
    head_count = query_block.shape[3]
    slab_width = math.gcd(4, head_count)

    def head_slab(slab_index):
        query_slab = lax.dynamic_slice_in_dim(query_block, slab_index * slab_width, slab_width, 3)
        return attend(query_slab, key_block, allowed, with_sink)

    stacked = lax.map(head_slab, jnp.arange(head_count // slab_width, dtype=jnp.int32))
    stacked = jnp.moveaxis(stacked, 0, 3)
    return stacked.reshape(stacked.shape[:3] + (head_count, stacked.shape[-1]))


def compress_blocks(keys_values, pos_weight, compress_weight):
    block_count = keys_values.shape[0] // BLOCK
    grouped = keys_values.reshape(block_count, BLOCK, GROUPS, 2 * HEAD_DIM).astype(jnp.float32)
    pooled = jnp.sum(grouped * pos_weight.astype(jnp.float32)[None, :, None, :], axis=1).astype(
        jnp.bfloat16
    )
    mapped = jnp.dot(
        pooled.reshape(block_count * GROUPS, 2 * HEAD_DIM),
        compress_weight,
        preferred_element_type=jnp.float32,
    )
    return mapped.astype(jnp.bfloat16).reshape(block_count, GROUPS, 2 * HEAD_DIM)


def plan_requests(unit_of, key_of, wanted, unit_count, key_count):
    hits = (
        wanted[:, None, None]
        & (unit_of[:, None, None] == jnp.arange(unit_count, dtype=jnp.int32)[None, :, None])
        & (key_of[:, None, None] == jnp.arange(key_count, dtype=jnp.int32)[None, None, :])
    )
    present = jnp.any(hits, axis=0)
    ordinal = jnp.cumsum(present.astype(jnp.int32), axis=1) - 1
    slot_of = jnp.sum(jnp.where(hits, ordinal[None], 0), axis=(1, 2))
    matches = present[:, :, None] & (
        ordinal[:, :, None] == jnp.arange(CAP, dtype=jnp.int32)[None, None, :]
    )
    requests = (
        jnp.sum(
            jnp.where(matches, jnp.arange(key_count, dtype=jnp.int32)[None, :, None] + 1, 0), axis=1
        )
        - 1
    )
    return (slot_of, requests)


def shards(queries, keys_values, selection, gate_logits, pos_weight, compress_weight):
    grp_index = lax.axis_index("grp")
    seq_index = lax.axis_index("seq")
    grp_count = lax.axis_size("grp")
    seq_count = lax.axis_size("seq")
    tok_count = queries.shape[0]
    dev_blocks = tok_count // BLOCK
    seg_tokens = tok_count * seq_count
    seg_blocks = seg_tokens // BLOCK
    all_blocks = seg_blocks * grp_count
    key_count = GROUPS * dev_blocks
    first_pos = (grp_index * seq_count + seq_index) * tok_count
    positions = first_pos + jnp.arange(tok_count, dtype=jnp.int32)
    local_view = keys_values.reshape(dev_blocks, BLOCK, GROUPS, 2 * HEAD_DIM)
    local_summary = jnp.transpose(
        compress_blocks(keys_values, pos_weight, compress_weight), (1, 0, 2)
    )
    summaries = lax.all_gather(local_summary, ("grp", "seq"), axis=1, tiled=True)
    picked = selection.reshape(dev_blocks, GROUPS, TOP)
    group_ids = jnp.broadcast_to(jnp.arange(GROUPS, dtype=jnp.int32)[None, :, None], picked.shape)
    flat_groups = group_ids.reshape(-1)
    flat_picks = picked.reshape(-1)
    clipped_flat = jnp.maximum(flat_picks, 0)
    segment_of = clipped_flat // seg_blocks
    key_of = flat_groups * dev_blocks + clipped_flat % dev_blocks
    wanted = (flat_picks >= 0) & (segment_of != grp_index)
    slot_of, requests = plan_requests(segment_of, key_of, wanted, grp_count, key_count)
    asked_clipped = jnp.maximum(
        lax.all_to_all(requests, "grp", split_axis=0, concat_axis=0, tiled=True), 0
    )
    received = lax.all_to_all(
        local_view[asked_clipped % dev_blocks, :, asked_clipped // dev_blocks, :],
        "grp",
        split_axis=0,
        concat_axis=0,
        tiled=True,
    )
    picks_clipped = jnp.maximum(picked, 0)
    pick_segment = picks_clipped // seg_blocks
    from_remote = received[pick_segment, slot_of.reshape(picked.shape)]
    segment = lax.all_gather(keys_values, "seq", axis=0, tiled=True)
    earlier_tail = from_behind(segment[seg_tokens - WINDOW :], "grp", 1)
    segment_view = segment.reshape(seg_blocks, BLOCK, GROUPS, 2 * HEAD_DIM)
    from_segment = segment_view[picks_clipped % seg_blocks, :, group_ids, :]
    start_row = jnp.maximum(seq_index * tok_count - WINDOW, 0)
    inside = lax.dynamic_slice_in_dim(segment, start_row, WINDOW, 0)
    before = jnp.where(seq_index == 0, earlier_tail, inside)
    own_rows = (pick_segment == grp_index)[..., None, None]
    chosen = jnp.where(own_rows, from_segment, from_remote).reshape(
        dev_blocks, GROUPS, TOP * BLOCK, 2 * HEAD_DIM
    )
    key_positions = (picks_clipped[..., None] * BLOCK + jnp.arange(BLOCK, dtype=jnp.int32)).reshape(
        dev_blocks, GROUPS, TOP * BLOCK
    )
    live_keys = jnp.repeat(picked >= 0, BLOCK, axis=2)
    block_positions = positions.reshape(dev_blocks, BLOCK)
    allowed_sel = live_keys[:, :, None, :] & (
        key_positions[:, :, None, :] <= block_positions[:, None, :, None]
    )
    query_blocks = queries.reshape(dev_blocks, BLOCK, GROUPS, GROUP_HEADS, HEAD_DIM)
    selected_branch = by_heads(query_blocks, chosen, allowed_sel, False).reshape(
        tok_count, GROUPS, GROUP_HEADS, HEAD_DIM
    )
    query_whole = queries.reshape(1, tok_count, GROUPS, GROUP_HEADS, HEAD_DIM)
    block_ends = jnp.arange(all_blocks, dtype=jnp.int32) * BLOCK + BLOCK - 1
    allowed_comp = (block_ends[None, :] <= positions[:, None])[None, None]
    compressed_branch = by_heads(query_whole, summaries[None], allowed_comp, True)[0]
    nearby = jnp.concatenate([before, keys_values], axis=0).reshape(
        WINDOW + tok_count, GROUPS, 2 * HEAD_DIM
    )
    nearby = jnp.transpose(nearby, (1, 0, 2))[None]
    near_positions = first_pos - WINDOW + jnp.arange(WINDOW + tok_count, dtype=jnp.int32)
    allowed_win = (
        (near_positions[None, :] <= positions[:, None])
        & (near_positions[None, :] > positions[:, None] - WINDOW)
        & (near_positions[None, :] >= 0)
    )[None, None]
    window_branch = by_heads(query_whole, nearby, allowed_win, False)[0]
    gate_values = jax.nn.sigmoid(gate_logits.astype(jnp.float32)).reshape(
        3, tok_count, GROUPS, GROUP_HEADS, 1
    )
    attended = (
        gate_values[0] * compressed_branch
        + gate_values[1] * selected_branch
        + gate_values[2] * window_branch
    )
    return attended.reshape(tok_count, HEADS * HEAD_DIM).astype(jnp.bfloat16)


def solution(mesh):
    in_specs = (
        P(("grp", "seq"), None),
        P(("grp", "seq"), None),
        P(("grp", "seq"), None),
        P(None, ("grp", "seq"), None),
        P(),
        P(),
    )
    out_specs = P(("grp", "seq"), None)
    return jax.shard_map(shards, mesh=mesh, in_specs=in_specs, out_specs=out_specs, check_vma=False)
```

profile of v0, /device:TPU:0, one launch (start us, length us, event | category | flops | bytes accessed | tf_op | source)
XLA Modules:
  0.0 216.7 jit_solution(13625318544058351301)
XLA Ops:
  6.5 1.3 broadcast_multiply_fusion
  10.9 6.3 %all-to-all-start = ((s32[4,1,2]{2,1,0:T(1,128)}), s32[4,1,2]{2,1,0:T(1,128)}, u32[]{:S(2)}, u32[]{:S(2)}) async-start(s32[4,1,2]{2,1,0:T(1,128)} %copy.101), calls=%async_computation | async-start | bytes 4096 | tf_op jit(solution)/shard_map/all_to_all | solution.py:134
  18.9 2.6 %copy.97 = bf16[128,6144]{0,1:T(8,128)(2,1)} copy(bf16[128,6144]{1,0:T(8,128)(2,1)} %param.12) | data formatting | bytes 3145728 | tf_op args[0]
  22.0 42.4 %all_gather.6 = bf16[2,64,384]{2,0,1:T(2,128)(2,1)S(1)} all-gather(bf16[2,2,384]{2,0,1:T(2,128)(2,1)S(1)} %bitcast.261), channel_id=1, replica_groups=mesh['grp'=4,'seq'=8] {'grp','seq'}, dimensions={1}, use_global_device_ids=true | all-gather | bytes 101376 | tf_op jit(solution)/shard_map/all_gather | solution.py:123
  65.3 14.9 %while.33 = (s32[]{:T(128)}, f32[4,1,128,2,4,192]{2,5,4,0,3,1:T(8,128)S(1)}, s32[4]{0:T(128)}, bf16[1,128,2,16,192]{1,4,3,2,0:T(8,128)(2,1)}, bf16[1,2,64,384]{3...) while((s32[]{:T(128)}, ...), condition=%wide.region_4.5_spmd.clone, body=%wide.region_1.4_spmd.clone.sunk | while | flops 51128324 | bytes 2171823 | solution.py:66
  65.3 1.3 dynamic_slice.50
  69.0 1.3 dynamic_slice.50
  80.3 1.8 copy.106
  87.3 2.3 %gather_fusion.1 = bf16[8,64,384]{2,1,0:T(8,128)(2,1)} fusion(bf16[2,64,2,384]{3,1,2,0:T(8,128)(2,1)} %copy.106, s32[8]{0:T(128)S(1)} %reshape.547), kind=kCustom, calls=%fused_computation.1 | custom fusion | bytes 786496 | tf_op jit(solution)/shard_map/gather | solution.py:137
  89.6 3.5 %all-to-all-start.1 = ((bf16[4,2,64,384]{3,2,1,0:T(8,128)(2,1)}), bf16[4,2,64,384]{3,2,1,0:T(8,128)(2,1)S(1)}, u32[]{:S(2)}, u32[]{:S(2)}) async-start(bf16[4,2,64,384]{3,2,1,0:T(8,128)(2,1)} %bitcast.255), calls=%async_computation.1 | async-start | bytes 786432 | tf_op jit(solution)/shard_map/all_to_all | solution.py:136
  93.8 4.7 %reshape.537 = bf16[2,64,2,16,192]{4,3,2,1,0:T(8,128)(2,1)} reshape(bf16[128,6144]{1,0:T(8,128)(2,1)} %param.12) | data formatting | bytes 3145728 | tf_op jit(solution)/shard_map/reshape | solution.py:165
  99.1 6.4 %all-to-all-done.1 = bf16[4,2,64,384]{3,2,1,0:T(8,128)(2,1)S(1)} async-done(((bf16[4,2,64,384]{3,2,1,0:T(8,128)(2,1)}), bf16[4,2,64,384]{3,2,1,0:T(8,128)(2,1)S(1)}, u32[]{:S(2)}, u32[]{:S(2)}) %all-to-all-start.1) | async-done | bytes 393248 | tf_op jit(solution)/shard_map/all_to_all | solution.py:136
  105.5 2.7 %gather_fusion.2 = bf16[64,64,384]{2,1,0:T(8,128)(2,1)} fusion(bf16[4,2,64,384]{3,2,1,0:T(8,128)(2,1)S(1)} %all-to-all-done.1, s32[64]{0:T(128)S(1)} %reshape.553), kind=kCustom, calls=%fused_computation.2 | custom fusion | bytes 6291968 | tf_op jit(solution)/shard_map/gather | solution.py:145
  108.2 3.4 %reshape.538 = bf16[16,64,2,384]{3,2,1,0:T(2,128)(2,1)S(1)} reshape(bf16[1024,768]{1,0:T(8,128)(2,1)} %all-gather.2.cloned.1.call-done) | data formatting | bytes 3145728 | tf_op jit(solution)/shard_map/reshape | solution.py:148
  111.9 2.7 %gather_fusion = bf16[64,64,384]{2,1,0:T(8,128)(2,1)} fusion(bf16[16,64,2,384]{3,1,2,0:T(8,128)(2,1)S(1)} %copy.100, s32[64]{0:T(128)S(1)} %reshape.541), kind=kCustom, calls=%fused_computation | custom fusion | bytes 6291968 | tf_op jit(solution)/shard_map/gather | solution.py:149
  114.6 4.4 %broadcast_select_fusion = bf16[2,2,1024,384]{3,2,1,0:T(8,128)(2,1)} fusion(bf16[2,2,1024,384]{3,2,1,0:T(8,128)(2,1)} %bitcast.253, bf16[2,2,1024,384]{3,2,1,0:T(8,128)(2,1)} %bitcast.252, pred[2,2,1024]{2,1,0:T(4,128)(4,1)S(1)} %broadcast_in_dim.161), kind=kLoop, calls=%fused_computation.84 | loop fusion | flops 1572864 | bytes 9441280 | tf_op jit(solution)/shard_map/jit(_where)/select_n | solution.py:154
  119.0 3.2 %copy.108 = bf16[2,2,1024,384]{2,3,1,0:T(8,128)(2,1)S(1)} copy(bf16[2,2,1024,384]{3,2,1,0:T(8,128)(2,1)} %broadcast_select_fusion) | data formatting | bytes 6291456
  122.2 1.6 slice.52
  123.8 2.1 collective-permute-start
  125.9 30.6 %while.34 = (s32[]{:T(128)}, f32[4,2,64,2,4,192]{5,2,4,3,1,0:T(8,128)}, s32[4]{0:T(128)S(1)}, bf16[2,64,2,16,192]{4,3,2,1,0:T(8,128)(2,1)}, bf16[2,2,1024,384]{2...) while((s32[]{:T(128)}, ...), condition=%wide.region_12.13_spmd.clone, body=%wide.region_9.12_spmd.clone.sunk | while | flops 814416896 | bytes 18646196 | solution.py:66
  127.1 1.5 constant_dynamic-slice_fusion.2
  129.6 2.1 fusion.132
  131.8 1.7 fusion.133
  134.8 1.5 constant_dynamic-slice_fusion.2
  137.3 2.1 fusion.132
  139.4 1.7 fusion.133
  142.4 1.5 constant_dynamic-slice_fusion.2
  144.9 2.1 fusion.132
  147.0 1.8 fusion.133
  150.1 1.5 constant_dynamic-slice_fusion.2
  152.6 2.1 fusion.132
  154.7 1.7 fusion.133
  156.4 11.7 %copy.121 = f32[2,64,2,4,4,192]{1,0,5,4,3,2:T(2,128)} copy(f32[2,64,2,4,4,192]{5,1,4,2,0,3:T(8,128)} %bitcast.16) | data formatting | bytes 6291456 | tf_op jit(solution)/shard_map/reshape;reshape | solution.py:166
  168.1 5.8 %reshape.575 = f32[128,6144]{0,1:T(8,128)S(1)} reshape(f32[2,64,2,4,4,192]{1,0,5,4,3,2:T(2,128)} %copy.121) | data formatting | bytes 6291456 | tf_op jit(solution)/shard_map/reshape;reshape | solution.py:166
  175.1 1.7 pad_maximum_fusion
  176.8 1.9 copy.111
  178.7 2.0 broadcast.656.clone2
  180.7 21.9 %while.35 = (s32[]{:T(128)}, f32[4,1,128,2,4,192]{2,5,4,0,3,1:T(8,128)}, s32[4]{0:T(128)S(1)}, bf16[1,128,2,16,192]{1,4,3,2,0:T(8,128)(2,1)}, bf16[1,2,256,384]{...) while((s32[]{:T(128)}, ...), condition=%wide.region_16.17_spmd.clone, body=%wide.region_13.16_spmd.clone.sunk | while | flops 204011520 | bytes 4873147 | solution.py:66
  182.0 1.5 fusion.136
  184.0 2.2 %fusion.138 = f32[4,1,128,2,4,192]{2,5,4,0,3,1:T(8,128)} fusion(f32[4,1,128,2,4,192]{2,5,4,0,3,1:T(8,128)} %get-tuple-element.488, s32[]{:T(128)} %get-tuple-element.487, f32[1,2,4,128,256]{4,3,2,1,0:T(8,128)S(1)} %get-tuple-element.472, f32[2,4,128]{2,1,0:T(4,128)S(1)} %get-tuple-element.473, pred[128,256]{1,0:T(8,128)(4,1)S(1)} %and_and_fusion.2, ...), kind=kOutput, calls=%fused_computation.60.clone.1 | convolution fusion | flops 101646336 | bytes 2073088 | tf_op jit(solution)/shard_map/while/body/eval_jaxpr/bghtn,bgnd->bghtd/dot_general | solution.py:47
  187.5 1.5 fusion.136
  189.4 2.2 %fusion.138 = f32[4,1,128,2,4,192]{2,5,4,0,3,1:T(8,128)} fusion(f32[4,1,128,2,4,192]{2,5,4,0,3,1:T(8,128)} %get-tuple-element.488, s32[]{:T(128)} %get-tuple-element.487, f32[1,2,4,128,256]{4,3,2,1,0:T(8,128)S(1)} %get-tuple-element.472, f32[2,4,128]{2,1,0:T(4,128)S(1)} %get-tuple-element.473, pred[128,256]{1,0:T(8,128)(4,1)S(1)} %and_and_fusion.2, ...), kind=kOutput, calls=%fused_computation.60.clone.1 | convolution fusion | flops 101646336 | bytes 2073088 | tf_op jit(solution)/shard_map/while/body/eval_jaxpr/bghtn,bgnd->bghtd/dot_general | solution.py:47
  193.0 1.5 fusion.136
  194.9 2.2 %fusion.138 = f32[4,1,128,2,4,192]{2,5,4,0,3,1:T(8,128)} fusion(f32[4,1,128,2,4,192]{2,5,4,0,3,1:T(8,128)} %get-tuple-element.488, s32[]{:T(128)} %get-tuple-element.487, f32[1,2,4,128,256]{4,3,2,1,0:T(8,128)S(1)} %get-tuple-element.472, f32[2,4,128]{2,1,0:T(4,128)S(1)} %get-tuple-element.473, pred[128,256]{1,0:T(8,128)(4,1)S(1)} %and_and_fusion.2, ...), kind=kOutput, calls=%fused_computation.60.clone.1 | convolution fusion | flops 101646336 | bytes 2073088 | tf_op jit(solution)/shard_map/while/body/eval_jaxpr/bghtn,bgnd->bghtd/dot_general | solution.py:47
  198.4 1.5 fusion.136
  200.4 2.3 %fusion.138 = f32[4,1,128,2,4,192]{2,5,4,0,3,1:T(8,128)} fusion(f32[4,1,128,2,4,192]{2,5,4,0,3,1:T(8,128)} %get-tuple-element.488, s32[]{:T(128)} %get-tuple-element.487, f32[1,2,4,128,256]{4,3,2,1,0:T(8,128)S(1)} %get-tuple-element.472, f32[2,4,128]{2,1,0:T(4,128)S(1)} %get-tuple-element.473, pred[128,256]{1,0:T(8,128)(4,1)S(1)} %and_and_fusion.2, ...), kind=kOutput, calls=%fused_computation.60.clone.1 | convolution fusion | flops 101646336 | bytes 2073088 | tf_op jit(solution)/shard_map/while/body/eval_jaxpr/bghtn,bgnd->bghtd/dot_general | solution.py:47
  202.6 4.6 %fusion.84 = bf16[128,6144]{0,1:T(8,128)(2,1)} fusion(f32[4,1,128,2,4,192]{2,5,4,0,3,1:T(8,128)} %get-tuple-element.103, f32[4,1,128,2,4,192]{2,5,4,0,3,1:T(8,128)} %copy-done.1, f32[128,6144]{0,1:T(8,128)S(1)} %reshape.575, f32[128,2,16]{0,2,1:T(8,128)S(1)} %bitcast.259, f32[128,2,16]{0,2,1:T(8,128)S(1)} %bitcast.260, f32[128,2,16]{0,2,1:T(8,128)S(1)} %bitcast.258), kind=kLoop, calls=%fused_computation.80 | loop fusion | flops 4718592 | bytes 11059200 | tf_op jit(solution)/shard_map/convert_element_type | solution.py:192
  207.3 2.6 %copy.113 = bf16[128,6144]{1,0:T(8,128)(2,1)} copy(bf16[128,6144]{0,1:T(8,128)(2,1)} %fusion.84) | data formatting | bytes 3145728 | tf_op jit(solution)/shard_map/convert_element_type | solution.py:192
  (139 shorter events, 34.4 us)
Async XLA Ops:
  6.5 15.3 %copy-start = (bf16[384,384]{1,0:T(8,128)(2,1)S(1)}, bf16[384,384]{1,0:T(8,128)(2,1)}, u32[]{:S(2)}) copy-start(bf16[384,384]{1,0:T(8,128)(2,1)} %param.17) | copy-start | bytes 884740
  6.5 15.0 %copy-start.3 = (bf16[64,384]{1,0:T(8,128)(2,1)S(1)}, bf16[64,384]{1,0:T(8,128)(2,1)}, u32[]{:S(2)}) copy-start(bf16[64,384]{1,0:T(8,128)(2,1)} %param.16) | copy-start | bytes 147460
  9.1 8.1 %copy-start.7 = (pred[2,32]{1,0:T(4,128)(4,1)}, pred[2,32]{1,0:T(4,128)(4,1)S(1)}, u32[]{:S(2)}) copy-start(pred[2,32]{1,0:T(4,128)(4,1)S(1)} %get-tuple-element.310) | copy-start | bytes 196
  9.1 8.1 %copy-start.8 = (pred[2,32]{1,0:T(4,128)(4,1)}, pred[2,32]{1,0:T(4,128)(4,1)S(1)}, u32[]{:S(2)}) copy-start(pred[2,32]{1,0:T(4,128)(4,1)S(1)} %get-tuple-element.293) | copy-start | bytes 196
  9.5 0.5 copy-start.5
  9.5 12.5 %copy-start.6 = (pred[64,4]{0,1:T(4,128)(4,1)}, pred[64,4]{0,1:T(4,128)(4,1)S(1)}, u32[]{:S(2)}) copy-start(pred[64,4]{0,1:T(4,128)(4,1)S(1)} %get-tuple-element.312) | copy-start | bytes 772
  10.9 75.5 %all-to-all-start = ((s32[4,1,2]{2,1,0:T(1,128)}), s32[4,1,2]{2,1,0:T(1,128)}, u32[]{:S(2)}, u32[]{:S(2)}) async-start(s32[4,1,2]{2,1,0:T(1,128)} %copy.101), calls=%async_computation | async-start | bytes 4096 | tf_op jit(solution)/shard_map/all_to_all | solution.py:134
  17.2 91.0 %all-gather.2.cloned.1.call-start = ((), (), s32[]{:S(2)}) async-start(), calls=%async_computation.2 | async-start | bytes 1769472 | tf_op jit(solution)/shard_map/all_gather | solution.py:146
  18.9 45.5 %copy-start.2 = (bf16[2,64,2,384]{3,2,1,0:T(2,128)(2,1)}, bf16[2,64,2,384]{3,2,1,0:T(2,128)(2,1)S(1)}, u32[]{:S(2)}) copy-start(bf16[2,64,2,384]{3,2,1,0:T(2,128)(2,1)S(1)} %reshape.535) | copy-start | bytes 589828
  80.2 9.4 %copy-start.1 = (f32[4,1,128,2,4,192]{2,5,4,0,3,1:T(8,128)}, f32[4,1,128,2,4,192]{2,5,4,0,3,1:T(8,128)S(1)}, u32[]{:S(2)}) copy-start(f32[4,1,128,2,4,192]{2,5,4,0,3,1:T(8,128)S(1)} %get-tuple-element.101) | copy-start | bytes 9437188
  80.2 18.9 %copy-start.4 = (bf16[3,128,32]{1,2,0:T(8,128)(2,1)S(1)}, bf16[3,128,32]{1,2,0:T(8,128)(2,1)}, u32[]{:S(2)}) copy-start(bf16[3,128,32]{1,2,0:T(8,128)(2,1)} %param.15) | copy-start | bytes 73732
  89.6 15.9 %all-to-all-start.1 = ((bf16[4,2,64,384]{3,2,1,0:T(8,128)(2,1)}), bf16[4,2,64,384]{3,2,1,0:T(8,128)(2,1)S(1)}, u32[]{:S(2)}, u32[]{:S(2)}) async-start(bf16[4,2,64,384]{3,2,1,0:T(8,128)(2,1)} %bitcast.255), calls=%async_computation.1 | async-start | bytes 786432 | tf_op jit(solution)/shard_map/all_to_all | solution.py:136
  123.8 50.2 %collective-permute-start = (bf16[128,768]{1,0:T(8,128)(2,1)}, bf16[128,768]{1,0:T(8,128)(2,1)}, u32[]{:S(2)}, u32[]{:S(2)}) collective-permute-start(bf16[128,768]{1,0:T(8,128)(2,1)} %slice.52), channel_id=1, source_target_pairs={{0,8},{8,16},{16,24},{1,9},{9,17},{17,25},{2,10},{10,18},{18,26},{... | collective-permute-start | bytes 589832 | tf_op jit(solution)/shard_map/ppermute | solution.py:21
Sparse Core Ops, SparseCore 0:
  19.9 27.4 all-gather.1
where the time goes:
time: 218 us; the launch traced here: 217 us
  local copies, waits for them, and re-layouts  74.2 us (34%)
  blocking collectives  42.4 us (19%)
  matrix products  31.7 us (15%)
  other arithmetic  28.2 us (13%)
  between operations  13.7 us (6%)
  starting transfers between devices  11.9 us (5%)
  loops' own time  7.63 us (4%)
  waiting for transfers between devices  7.09 us (3%)
    all_gather x1, blocking collectives, shards(): lax.all_gather(local_summary, ('grp', 'seq'), axis=1, tiled=True)  42.4 us
    dot_general x12, matrix products, attend(): jnp.einsum('bghtn,bgnd->bghtd', rounded, key_block[..., head_dim:], prefe...  17.7 us
    another operation x2, local copies, waits for them, and re-layouts, shards(): by_heads(query_blocks, chosen, allowed_sel, False)  17.5 us
    dot_general x12, matrix products, attend(): jnp.einsum('btghd,bgnd->bghtn', query_block, key_block[..., :head_dim], p...  13.8 us
    dynamic_slice x12, local copies, waits for them, and re-layouts, by_heads(): lax.map(head_slab, jnp.arange(head_count // slab_width, dtype=jnp.int32))  9.99 us
    sub x4, other arithmetic, attend(): weights = jnp.where(allowed_wide, jnp.exp(scores - top_score), 0.0)  8.59 us
    another operation x3, loops' own time, by_heads(): lax.map(head_slab, jnp.arange(head_count // slab_width, dtype=jnp.int32))  7.63 us
    all_to_all x1, waiting for transfers between devices, shards(): lax.all_to_all(local_view[asked_clipped % dev_blocks, :, asked_clipped //...  6.38 us
  transfers between devices with their start and end apart: 4, of which 1 were waited for; matrix products, arithmetic and copies ran while one was open for 37% of the time, Pallas kernels for 0%

commit v1 on v0

--- a/solution.py
+++ b/solution.py
@@ -13,6 +13,29 @@
 CAP = 2
 WINDOW = 128
 NEG_FILL = -1e30
+
+
+def cut_along(x, dim, size):
+    shape = x.shape
+    blocks = x.reshape(*shape[:dim], size, shape[dim] // size, *shape[dim + 1 :])
+    return jnp.moveaxis(blocks, dim, 0)
+
+
+def joined_along(blocks, dim):
+    lengths = list(blocks.shape[1:])
+    lengths[dim] *= blocks.shape[0]
+    return jnp.moveaxis(blocks, 0, dim).reshape(lengths)
+
+
+def pairwise_exchange(x, axis, split_dim, concat_dim):
+    size, index = (lax.axis_size(axis), lax.axis_index(axis))
+    blocks = cut_along(x, split_dim, size)
+    outs = [blocks[index]]
+    for step in range(1, size):
+        sent = blocks[index ^ step]
+        outs.append(lax.ppermute(sent, axis, [(i, i ^ step) for i in range(size)]))
+    blocks = jnp.stack(outs)[index ^ jnp.arange(size)]
+    return joined_along(blocks, concat_dim)
 
 
 def from_behind(block, axis, distance):
@@ -130,9 +153,7 @@
     key_of = flat_groups * dev_blocks + clipped_flat % dev_blocks
     wanted = (flat_picks >= 0) & (segment_of != grp_index)
     slot_of, requests = plan_requests(segment_of, key_of, wanted, grp_count, key_count)
-    asked_clipped = jnp.maximum(
-        lax.all_to_all(requests, "grp", split_axis=0, concat_axis=0, tiled=True), 0
-    )
+    asked_clipped = jnp.maximum(pairwise_exchange(requests, "grp", 0, 0), 0)
     received = lax.all_to_all(
         local_view[asked_clipped % dev_blocks, :, asked_clipped // dev_blocks, :],
         "grp",

time: 218 us -> 223 us (1.023)
  other arithmetic: 28.2 us -> 31.9 us
    all_to_all x1 -> x0, starting transfers between devices: 6.32 us -> none  [shards(): lax.all_to_all(requests, 'grp', split_axis=0, concat_axis=0, tiled=True)]
    ppermute x0 -> x3, starting transfers between devices: none -> 5.62 us  [pairwise_exchange(): outs.append(lax.ppermute(sent, axis, [(i, i ^ step) for i in range(size)]))]
    ppermute x0 -> x3, other arithmetic: none -> 2.38 us  [pairwise_exchange(): outs.append(lax.ppermute(sent, axis, [(i, i ^ step) for i in range(size)]))]
  transfers between devices with their start and end apart: 4 -> 6, of which waited for: 1 -> 1; matrix products, arithmetic and copies ran while one was open for 37% -> 41% of each run, Pallas kernels for 0% -> 0%
where the time goes in v1:
time: 223 us; the launch traced here: 221 us
  local copies, waits for them, and re-layouts  75.4 us (34%)
  blocking collectives  42.4 us (19%)
  other arithmetic  31.9 us (14%)
  matrix products  31.6 us (14%)
  between operations  13.8 us (6%)
  starting transfers between devices  11.2 us (5%)
  loops' own time  7.62 us (3%)
  waiting for transfers between devices  7.11 us (3%)
    all_gather x1, blocking collectives, shards(): lax.all_gather(local_summary, ('grp', 'seq'), axis=1, tiled=True)  42.4 us
    dot_general x12, matrix products, attend(): jnp.einsum('bghtn,bgnd->bghtd', rounded, key_block[..., head_dim:], prefe...  17.7 us
    another operation x2, local copies, waits for them, and re-layouts, shards(): by_heads(query_blocks, chosen, allowed_sel, False)  17.5 us
    dot_general x12, matrix products, attend(): jnp.einsum('btghd,bgnd->bghtn', query_block, key_block[..., :head_dim], p...  13.8 us
    dynamic_slice x12, local copies, waits for them, and re-layouts, by_heads(): lax.map(head_slab, jnp.arange(head_count // slab_width, dtype=jnp.int32))  9.94 us
    sub x4, other arithmetic, attend(): weights = jnp.where(allowed_wide, jnp.exp(scores - top_score), 0.0)  8.59 us
    another operation x3, loops' own time, by_heads(): lax.map(head_slab, jnp.arange(head_count // slab_width, dtype=jnp.int32))  7.62 us
    all_to_all x1, waiting for transfers between devices, shards(): lax.all_to_all(local_view[asked_clipped % dev_blocks, :, asked_clipped //...  6.38 us
  transfers between devices with their start and end apart: 6, of which 1 were waited for; matrix products, arithmetic and copies ran while one was open for 41% of the time, Pallas kernels for 0%

profile of v1, /device:TPU:0, one launch (start us, length us, event | category | flops | bytes accessed | tf_op | source)
XLA Modules:
  0.0 221.0 jit_solution(15610906751082634305)
XLA Ops:
  7.3 1.3 broadcast_multiply_fusion
  10.7 1.4 fusion.94
  12.1 3.0 %collective-permute-start = (s32[1,2]{0,1:T(2,128)}, s32[1,2]{0,1:T(2,128)}, u32[]{:S(2)}, u32[]{:S(2)}) collective-permute-start(s32[1,2]{0,1:T(2,128)} %get-tuple-element.300), channel_id=1, source_target_pairs={{0,8},{8,0},{16,24},{24,16},{1,9},{9,1},{17,25},{25,17},{2,10},{10... | collective-permute-start | bytes 32 | tf_op jit(solution)/shard_map/ppermute | solution.py:36
  15.1 2.6 %collective-permute-start.1 = (s32[1,2]{0,1:T(2,128)}, s32[1,2]{0,1:T(2,128)}, u32[]{:S(2)}, u32[]{:S(2)}) collective-permute-start(s32[1,2]{0,1:T(2,128)} %get-tuple-element.299), channel_id=1, source_target_pairs={{0,16},{8,24},{16,0},{24,8},{1,17},{9,25},{17,1},{25,9},{2,18},{10... | collective-permute-start | bytes 32 | tf_op jit(solution)/shard_map/ppermute | solution.py:36
  18.8 2.6 %copy.91 = bf16[128,6144]{0,1:T(8,128)(2,1)} copy(bf16[128,6144]{1,0:T(8,128)(2,1)} %param.12) | data formatting | bytes 3145728 | tf_op args[0]
  21.9 42.4 %all_gather.6 = bf16[2,64,384]{2,0,1:T(2,128)(2,1)S(1)} all-gather(bf16[2,2,384]{2,0,1:T(2,128)(2,1)S(1)} %bitcast.261), channel_id=1, replica_groups=mesh['grp'=4,'seq'=8] {'grp','seq'}, dimensions={1}, use_global_device_ids=true | all-gather | bytes 101376 | tf_op jit(solution)/shard_map/all_gather | solution.py:146
  65.1 14.9 %while.33 = (s32[]{:T(128)}, f32[4,1,128,2,4,192]{2,5,4,0,3,1:T(8,128)S(1)}, s32[4]{0:T(128)}, bf16[1,128,2,16,192]{1,4,3,2,0:T(8,128)(2,1)}, bf16[1,2,64,384]{3...) while((s32[]{:T(128)}, ...), condition=%wide.region_4.5_spmd.clone, body=%wide.region_1.4_spmd.clone.sunk | while | flops 51128324 | bytes 2171823 | solution.py:89
  80.8 1.8 copy.101
  91.6 2.3 %gather_fusion.2 = bf16[8,64,384]{2,1,0:T(8,128)(2,1)} fusion(bf16[2,64,2,384]{3,1,2,0:T(8,128)(2,1)} %copy.101, s32[8]{0:T(128)S(1)} %reshape.571), kind=kCustom, calls=%fused_computation.2 | custom fusion | bytes 786496 | tf_op jit(solution)/shard_map/gather | solution.py:158
  93.9 3.5 %all-to-all-start = ((bf16[4,2,64,384]{3,2,1,0:T(8,128)(2,1)}), bf16[4,2,64,384]{3,2,1,0:T(8,128)(2,1)S(1)}, u32[]{:S(2)}, u32[]{:S(2)}) async-start(bf16[4,2,64,384]{3,2,1,0:T(8,128)(2,1)} %bitcast.254), calls=%async_computation | async-start | bytes 786432 | tf_op jit(solution)/shard_map/all_to_all | solution.py:157
  98.1 4.7 %reshape.551 = bf16[2,64,2,16,192]{4,3,2,1,0:T(8,128)(2,1)} reshape(bf16[128,6144]{1,0:T(8,128)(2,1)} %param.12) | data formatting | bytes 3145728 | tf_op jit(solution)/shard_map/reshape | solution.py:186
  103.4 6.4 %all-to-all-done = bf16[4,2,64,384]{3,2,1,0:T(8,128)(2,1)S(1)} async-done(((bf16[4,2,64,384]{3,2,1,0:T(8,128)(2,1)}), bf16[4,2,64,384]{3,2,1,0:T(8,128)(2,1)S(1)}, u32[]{:S(2)}, u32[]{:S(2)}) %all-to-all-start) | async-done | bytes 393248 | tf_op jit(solution)/shard_map/all_to_all | solution.py:157
  109.8 2.7 %gather_fusion.3 = bf16[64,64,384]{2,1,0:T(8,128)(2,1)} fusion(bf16[4,2,64,384]{3,2,1,0:T(8,128)(2,1)S(1)} %all-to-all-done, s32[64]{0:T(128)S(1)} %reshape.577), kind=kCustom, calls=%fused_computation.3 | custom fusion | bytes 6291968 | tf_op jit(solution)/shard_map/gather | solution.py:166
  112.5 3.4 %reshape.552 = bf16[16,64,2,384]{3,2,1,0:T(2,128)(2,1)S(1)} reshape(bf16[1024,768]{1,0:T(8,128)(2,1)} %all-gather.2.cloned.1.call-done) | data formatting | bytes 3145728 | tf_op jit(solution)/shard_map/reshape | solution.py:169
  116.2 2.7 %gather_fusion = bf16[64,64,384]{2,1,0:T(8,128)(2,1)} fusion(bf16[16,64,2,384]{3,1,2,0:T(8,128)(2,1)S(1)} %copy.94, s32[64]{0:T(128)S(1)} %reshape.555), kind=kCustom, calls=%fused_computation | custom fusion | bytes 6291968 | tf_op jit(solution)/shard_map/gather | solution.py:170
  118.9 4.4 %broadcast_select_fusion = bf16[2,2,1024,384]{3,2,1,0:T(8,128)(2,1)} fusion(bf16[2,2,1024,384]{3,2,1,0:T(8,128)(2,1)} %bitcast.252, bf16[2,2,1024,384]{3,2,1,0:T(8,128)(2,1)} %bitcast.251, pred[2,2,1024]{2,1,0:T(4,128)(4,1)S(1)} %broadcast_in_dim.162), kind=kLoop, calls=%fused_computation.85 | loop fusion | flops 1572864 | bytes 9441280 | tf_op jit(solution)/shard_map/jit(_where)/select_n | solution.py:175
  123.3 3.2 %copy.103 = bf16[2,2,1024,384]{2,3,1,0:T(8,128)(2,1)S(1)} copy(bf16[2,2,1024,384]{3,2,1,0:T(8,128)(2,1)} %broadcast_select_fusion) | data formatting | bytes 6291456
  126.5 1.6 slice.54
  128.1 2.1 collective-permute-start.3
  130.2 30.6 %while.34 = (s32[]{:T(128)}, f32[4,2,64,2,4,192]{5,2,4,3,1,0:T(8,128)}, s32[4]{0:T(128)S(1)}, bf16[2,64,2,16,192]{4,3,2,1,0:T(8,128)(2,1)}, bf16[2,2,1024,384]{2...) while((s32[]{:T(128)}, ...), condition=%wide.region_12.13_spmd.clone, body=%wide.region_9.12_spmd.clone.sunk | while | flops 814416896 | bytes 18646196 | solution.py:89
  131.5 1.5 constant_dynamic-slice_fusion.6
  133.9 2.1 fusion.134
  136.1 1.7 fusion.135
  139.1 1.5 constant_dynamic-slice_fusion.6
  141.6 2.1 fusion.134
  143.7 1.7 fusion.135
  146.7 1.5 constant_dynamic-slice_fusion.6
  149.2 2.1 fusion.134
  151.3 1.8 fusion.135
  154.4 1.5 constant_dynamic-slice_fusion.6
  156.9 2.1 fusion.134
  159.0 1.7 fusion.135
  160.8 11.7 %copy.116 = f32[2,64,2,4,4,192]{1,0,5,4,3,2:T(2,128)} copy(f32[2,64,2,4,4,192]{5,1,4,2,0,3:T(8,128)} %bitcast.17) | data formatting | bytes 6291456 | tf_op jit(solution)/shard_map/reshape;reshape | solution.py:187
  172.5 5.8 %reshape.611 = f32[128,6144]{0,1:T(8,128)S(1)} reshape(f32[2,64,2,4,4,192]{1,0,5,4,3,2:T(2,128)} %copy.116) | data formatting | bytes 6291456 | tf_op jit(solution)/shard_map/reshape;reshape | solution.py:187
  179.4 1.7 pad_maximum_fusion
  181.1 1.9 copy.106
  183.0 2.0 broadcast.674.clone2
  185.1 21.9 %while.35 = (s32[]{:T(128)}, f32[4,1,128,2,4,192]{2,5,4,0,3,1:T(8,128)}, s32[4]{0:T(128)S(1)}, bf16[1,128,2,16,192]{1,4,3,2,0:T(8,128)(2,1)}, bf16[1,2,256,384]{...) while((s32[]{:T(128)}, ...), condition=%wide.region_16.17_spmd.clone, body=%wide.region_13.16_spmd.clone.sunk | while | flops 204011520 | bytes 4873147 | solution.py:89
  186.4 1.5 fusion.138
  188.3 2.2 %fusion.140 = f32[4,1,128,2,4,192]{2,5,4,0,3,1:T(8,128)} fusion(f32[4,1,128,2,4,192]{2,5,4,0,3,1:T(8,128)} %get-tuple-element.479, s32[]{:T(128)} %get-tuple-element.478, f32[1,2,4,128,256]{4,3,2,1,0:T(8,128)S(1)} %get-tuple-element.463, f32[2,4,128]{2,1,0:T(4,128)S(1)} %get-tuple-element.464, pred[128,256]{1,0:T(8,128)(4,1)S(1)} %and_and_fusion.2, ...), kind=kOutput, calls=%fused_computation.61.clone.1 | convolution fusion | flops 101646336 | bytes 2073088 | tf_op jit(solution)/shard_map/while/body/eval_jaxpr/bghtn,bgnd->bghtd/dot_general | solution.py:70
  191.8 1.5 fusion.138
  193.8 2.2 %fusion.140 = f32[4,1,128,2,4,192]{2,5,4,0,3,1:T(8,128)} fusion(f32[4,1,128,2,4,192]{2,5,4,0,3,1:T(8,128)} %get-tuple-element.479, s32[]{:T(128)} %get-tuple-element.478, f32[1,2,4,128,256]{4,3,2,1,0:T(8,128)S(1)} %get-tuple-element.463, f32[2,4,128]{2,1,0:T(4,128)S(1)} %get-tuple-element.464, pred[128,256]{1,0:T(8,128)(4,1)S(1)} %and_and_fusion.2, ...), kind=kOutput, calls=%fused_computation.61.clone.1 | convolution fusion | flops 101646336 | bytes 2073088 | tf_op jit(solution)/shard_map/while/body/eval_jaxpr/bghtn,bgnd->bghtd/dot_general | solution.py:70
  197.3 1.5 fusion.138
  199.2 2.2 %fusion.140 = f32[4,1,128,2,4,192]{2,5,4,0,3,1:T(8,128)} fusion(f32[4,1,128,2,4,192]{2,5,4,0,3,1:T(8,128)} %get-tuple-element.479, s32[]{:T(128)} %get-tuple-element.478, f32[1,2,4,128,256]{4,3,2,1,0:T(8,128)S(1)} %get-tuple-element.463, f32[2,4,128]{2,1,0:T(4,128)S(1)} %get-tuple-element.464, pred[128,256]{1,0:T(8,128)(4,1)S(1)} %and_and_fusion.2, ...), kind=kOutput, calls=%fused_computation.61.clone.1 | convolution fusion | flops 101646336 | bytes 2073088 | tf_op jit(solution)/shard_map/while/body/eval_jaxpr/bghtn,bgnd->bghtd/dot_general | solution.py:70
  202.7 1.5 fusion.138
  204.7 2.3 %fusion.140 = f32[4,1,128,2,4,192]{2,5,4,0,3,1:T(8,128)} fusion(f32[4,1,128,2,4,192]{2,5,4,0,3,1:T(8,128)} %get-tuple-element.479, s32[]{:T(128)} %get-tuple-element.478, f32[1,2,4,128,256]{4,3,2,1,0:T(8,128)S(1)} %get-tuple-element.463, f32[2,4,128]{2,1,0:T(4,128)S(1)} %get-tuple-element.464, pred[128,256]{1,0:T(8,128)(4,1)S(1)} %and_and_fusion.2, ...), kind=kOutput, calls=%fused_computation.61.clone.1 | convolution fusion | flops 101646336 | bytes 2073088 | tf_op jit(solution)/shard_map/while/body/eval_jaxpr/bghtn,bgnd->bghtd/dot_general | solution.py:70
  207.0 4.6 %fusion.84 = bf16[128,6144]{0,1:T(8,128)(2,1)} fusion(f32[4,1,128,2,4,192]{2,5,4,0,3,1:T(8,128)} %get-tuple-element.103, f32[4,1,128,2,4,192]{2,5,4,0,3,1:T(8,128)} %copy-done.1, f32[128,6144]{0,1:T(8,128)S(1)} %reshape.611, f32[128,2,16]{0,2,1:T(8,128)S(1)} %bitcast.259, f32[128,2,16]{0,2,1:T(8,128)S(1)} %bitcast.260, f32[128,2,16]{0,2,1:T(8,128)S(1)} %bitcast.258), kind=kLoop, calls=%fused_computation.81 | loop fusion | flops 4718592 | bytes 11059200 | tf_op jit(solution)/shard_map/convert_element_type | solution.py:213
  211.6 2.6 %copy.108 = bf16[128,6144]{1,0:T(8,128)(2,1)} copy(bf16[128,6144]{0,1:T(8,128)(2,1)} %fusion.84) | data formatting | bytes 3145728 | tf_op jit(solution)/shard_map/convert_element_type | solution.py:213
  (154 shorter events, 40.6 us)
Async XLA Ops:
  6.5 15.1 %copy-start = (bf16[384,384]{1,0:T(8,128)(2,1)S(1)}, bf16[384,384]{1,0:T(8,128)(2,1)}, u32[]{:S(2)}) copy-start(bf16[384,384]{1,0:T(8,128)(2,1)} %param.17) | copy-start | bytes 884740
  6.5 14.9 %copy-start.3 = (bf16[64,384]{1,0:T(8,128)(2,1)S(1)}, bf16[64,384]{1,0:T(8,128)(2,1)}, u32[]{:S(2)}) copy-start(bf16[64,384]{1,0:T(8,128)(2,1)} %param.16) | copy-start | bytes 147460
  6.5 106.0 %all-gather.2.cloned.1.call-start = ((), (), s32[]{:S(2)}) async-start(), calls=%async_computation.1 | async-start | bytes 1769472 | tf_op jit(solution)/shard_map/all_gather | solution.py:167
  9.7 8.0 %copy-start.7 = (pred[2,32]{1,0:T(4,128)(4,1)}, pred[2,32]{1,0:T(4,128)(4,1)S(1)}, u32[]{:S(2)}) copy-start(pred[2,32]{1,0:T(4,128)(4,1)S(1)} %get-tuple-element.301) | copy-start | bytes 196
  9.7 8.0 %copy-start.8 = (pred[2,32]{1,0:T(4,128)(4,1)}, pred[2,32]{1,0:T(4,128)(4,1)S(1)}, u32[]{:S(2)}) copy-start(pred[2,32]{1,0:T(4,128)(4,1)S(1)} %get-tuple-element.278) | copy-start | bytes 196
  10.2 11.6 %copy-start.5 = (pred[64,4]{0,1:T(4,128)(4,1)}, pred[64,4]{0,1:T(4,128)(4,1)S(1)}, u32[]{:S(2)}) copy-start(pred[64,4]{0,1:T(4,128)(4,1)S(1)} %get-tuple-element.302) | copy-start | bytes 772
  10.2 11.6 %copy-start.6 = (pred[64,4]{0,1:T(4,128)(4,1)}, pred[64,4]{0,1:T(4,128)(4,1)S(1)}, u32[]{:S(2)}) copy-start(pred[64,4]{0,1:T(4,128)(4,1)S(1)} %get-tuple-element.303) | copy-start | bytes 772
  12.1 75.4 %collective-permute-start = (s32[1,2]{0,1:T(2,128)}, s32[1,2]{0,1:T(2,128)}, u32[]{:S(2)}, u32[]{:S(2)}) collective-permute-start(s32[1,2]{0,1:T(2,128)} %get-tuple-element.300), channel_id=1, source_target_pairs={{0,8},{8,0},{16,24},{24,16},{1,9},{9,1},{17,25},{25,17},{2,10},{10... | collective-permute-start | bytes 32 | tf_op jit(solution)/shard_map/ppermute | solution.py:36
  15.1 73.2 %collective-permute-start.1 = (s32[1,2]{0,1:T(2,128)}, s32[1,2]{0,1:T(2,128)}, u32[]{:S(2)}, u32[]{:S(2)}) collective-permute-start(s32[1,2]{0,1:T(2,128)} %get-tuple-element.299), channel_id=1, source_target_pairs={{0,16},{8,24},{16,0},{24,8},{1,17},{9,25},{17,1},{25,9},{2,18},{10... | collective-permute-start | bytes 32 | tf_op jit(solution)/shard_map/ppermute | solution.py:36
  17.7 71.4 %collective-permute-start.2 = (s32[1,2]{0,1:T(2,128)}, s32[1,2]{0,1:T(2,128)}, u32[]{:S(2)}, u32[]{:S(2)}) collective-permute-start(s32[1,2]{0,1:T(2,128)} %get-tuple-element.298), channel_id=1, source_target_pairs={{0,24},{8,16},{16,8},{24,0},{1,25},{9,17},{17,9},{25,1},{2,26},{10... | collective-permute-start | bytes 32 | tf_op jit(solution)/shard_map/ppermute | solution.py:36
  18.7 45.5 %copy-start.2 = (bf16[2,64,2,384]{3,2,1,0:T(2,128)(2,1)}, bf16[2,64,2,384]{3,2,1,0:T(2,128)(2,1)S(1)}, u32[]{:S(2)}) copy-start(bf16[2,64,2,384]{3,2,1,0:T(2,128)(2,1)S(1)} %reshape.549) | copy-start | bytes 589828
  80.0 14.0 %copy-start.1 = (f32[4,1,128,2,4,192]{2,5,4,0,3,1:T(8,128)}, f32[4,1,128,2,4,192]{2,5,4,0,3,1:T(8,128)S(1)}, u32[]{:S(2)}) copy-start(f32[4,1,128,2,4,192]{2,5,4,0,3,1:T(8,128)S(1)} %get-tuple-element.101) | copy-start | bytes 9437188
  80.0 23.4 %copy-start.4 = (bf16[3,128,32]{1,2,0:T(8,128)(2,1)S(1)}, bf16[3,128,32]{1,2,0:T(8,128)(2,1)}, u32[]{:S(2)}) copy-start(bf16[3,128,32]{1,2,0:T(8,128)(2,1)} %param.15) | copy-start | bytes 73732
  93.9 15.9 %all-to-all-start = ((bf16[4,2,64,384]{3,2,1,0:T(8,128)(2,1)}), bf16[4,2,64,384]{3,2,1,0:T(8,128)(2,1)S(1)}, u32[]{:S(2)}, u32[]{:S(2)}) async-start(bf16[4,2,64,384]{3,2,1,0:T(8,128)(2,1)} %bitcast.254), calls=%async_computation | async-start | bytes 786432 | tf_op jit(solution)/shard_map/all_to_all | solution.py:157
  128.1 50.2 %collective-permute-start.3 = (bf16[128,768]{1,0:T(8,128)(2,1)}, bf16[128,768]{1,0:T(8,128)(2,1)}, u32[]{:S(2)}, u32[]{:S(2)}) collective-permute-start(bf16[128,768]{1,0:T(8,128)(2,1)} %slice.54), channel_id=1, source_target_pairs={{0,8},{8,16},{16,24},{1,9},{9,17},{17,25},{2,10},{10,18},{18,26},{... | collective-permute-start | bytes 589832 | tf_op jit(solution)/shard_map/ppermute | solution.py:44
Sparse Core Ops, SparseCore 0:
  9.2 28.5 all-gather.1
